TPU v7x, 256 devices: a whole 4x4x8 slice. The times are simulated.
256 devices in a mesh: cols: 64 (over x, z, y_hi), sec: 4 (over y_lo, core).
Axes of the slice: x: 4, y: 4 (y_hi: 2, y_lo: 2; y = y_hi * 2 + y_lo), z: 8, core: 2. Of those that a mesh axis runs over, the one named last changes fastest.
Arguments:
- trial: float32 [128, 16, 96, 512], P('cols', None, None, 'sec'), may hold values from -6 to 6
- orbitals: float32 [64, 16, 96, 512], P('cols', None, None, 'sec'), may hold values from -6 to 6
- potential: float32 [16, 96, 512], P(None, None, 'sec'), may hold values from -4 to 4
- owner: int32 [2], replicated, may hold values from 0 to 63
Outputs:
- response: float32 [128, 16, 96, 512], P('cols', None, None, 'sec')
All inputs are finite; a program needn't handle non-finite values.
Results may differ from a plain program's by a relative error of at most 0.00002.
Values sent between devices are 32-bit elements; how exact they have to be, the bound alone decides.
A program may use at most 64 MiB of HBM per device.

v0:
```python
import jax
import jax.numpy as jnp
from jax import lax
from jax.sharding import PartitionSpec as P

ROUNDS = 2


grid_step = 0.5
spectrum_mid = 16.0
spectrum_half = 20.0
occupation = 2.0
weight_zero = 0.4
weight_one = -0.5
weight_two = 0.3
weight_three = -0.25


def with_halo(shard, sides, width):
    for axis, dim in sides:
        devices, length = (lax.axis_size(axis), shard.shape[dim])
        up = [(i, (i + 1) % devices) for i in range(devices)]
        down = [(j, i) for i, j in up]
        last = lax.slice_in_dim(shard, length - width, length, axis=dim)
        leading = lax.slice_in_dim(shard, 0, width, axis=dim)
        before = lax.ppermute(last, axis, up)
        after = lax.ppermute(leading, axis, down)
        shard = jnp.concatenate([before, shard, after], axis=dim)
    return shard


def broadcast(block, axis, holder):
    block = jnp.where(lax.axis_index(axis) == holder, block, jnp.zeros_like(block))
    return lax.psum(block, axis)


def apply_scaled(extended, potential):
    center = extended[..., 2:-2]
    diag_coef = -30.0 / 12.0
    near_coef = 16.0 / 12.0
    far_coef = -1.0 / 12.0
    along_x = (
        diag_coef * center
        + near_coef * (extended[..., 3:-1] + extended[..., 1:-3])
        + far_coef * (extended[..., 4:] + extended[..., :-4])
    )
    leading = center.ndim - 3
    padded = jnp.pad(center, [(0, 0)] * leading + [(2, 2), (2, 2), (0, 0)])
    along_y = (
        diag_coef * center
        + near_coef * (padded[..., 3:-1, 2:-2, :] + padded[..., 1:-3, 2:-2, :])
        + far_coef * (padded[..., 4:, 2:-2, :] + padded[..., :-4, 2:-2, :])
    )
    along_z = (
        diag_coef * center
        + near_coef * (padded[..., 2:-2, 3:-1, :] + padded[..., 2:-2, 1:-3, :])
        + far_coef * (padded[..., 2:-2, 4:, :] + padded[..., 2:-2, :-4, :])
    )
    kinetic = -0.5 * (along_x + along_y + along_z) / (grid_step * grid_step)
    return (kinetic + potential * center - spectrum_mid * center) / spectrum_half


def scaled_step(field, potential):
    extended = with_halo(field, (("sec", 3),), 2)
    return apply_scaled(extended, potential)


def fetch_orbital(orbitals, root):
    local = orbitals[0]
    return broadcast(local, "cols", root)


def body(trial, orbitals, potential, owner):
    total = jnp.zeros_like(trial)
    for turn in range(ROUNDS):
        orbital = fetch_orbital(orbitals, owner[turn])
        first = orbital[None] * trial
        second = scaled_step(first, potential)
        third = 2.0 * scaled_step(second, potential) - first
        fourth = 2.0 * scaled_step(third, potential) - second
        filtered = (
            weight_zero * first + weight_one * second + weight_two * third + weight_three * fourth
        )
        total = total + occupation * orbital[None] * filtered
    return total


def solution(mesh):
    placed = (P("cols", None, None, "sec"), P("cols", None, None, "sec"), P(None, None, "sec"), P())
    return jax.shard_map(
        body, mesh=mesh, in_specs=placed, out_specs=P("cols", None, None, "sec"), check_vma=False
    )
```

profile of v0, /device:TPU:1, one launch (start us, length us, event | category | flops | bytes accessed | tf_op | source)
XLA Modules:
  0.0 817.3 jit_solution(12986631056074869395)
XLA Ops:
  6.5 1.3 fusion.173
  9.1 2.5 select_bitcast_fusion.1
  11.5 3.0 copy.7
  14.5 0.5 copy.8
  15.1 1.4 copy.9
  16.5 651.8 %all-reduce.9.cloned.1.call-done = (f32[16,96,128]{2,1,0:T(8,128)}, f32[16,96,128]{2,1,0:T(8,128)}) async-done(((f32[16,96,128]{2,1,0:T(8,128)}, f32[16,96,128]{2,1,0:T(8,128)}), (f32[16,96,128]{2,1,0:T(8,128)}, f32[16,96,128]{2,1,0:T(8,128)})) %all-reduce.9.cloned.1.call-update) | async-done | bytes 1572880 | tf_op jit(solution)/shard_map/psum | solution.py:34
  668.3 2.6 copy.11
  670.9 1.4 copy.6
  672.2 2.4 broadcast_multiply_fusion.3
  674.7 47.2 %collective-permute-start = (f32[2,16,96,2]{2,1,3,0:T(8,128)S(1)}, f32[2,16,96,2]{2,1,3,0:T(8,128)S(1)}, u32[]{:S(2)}, u32[]{:S(2)}) collective-permute-start(f32[2,16,96,2]{2,1,3,0:T(8,128)S(1)} %get-tuple-element.15), channel_id=1, source_target_pairs={{1,0},{2,1},{3,2},{0,3},{5,4},{6,5},{7,6},{4,7},{9,8},{10,9},{11,1... | collective-permute-start | bytes 73736 | tf_op jit(solution)/shard_map/ppermute | solution.py:27
  721.9 0.2 collective-permute-start.1
  722.2 0.3 collective-permute-start.6
  722.5 1.5 collective-permute-start.7
  723.9 4.7 broadcast_multiply_fusion.2
  728.7 1.5 collective-permute-start.2
  730.2 0.5 collective-permute-start.3
  730.8 5.7 broadcast_multiply_fusion.1
  736.4 0.8 fusion.171
  737.3 0.7 collective-permute-start.8
  737.9 1.1 collective-permute-start.9
  739.0 14.8 %fusion.68 = f32[2,16,96,128]{2,1,3,0:T(8,128)} fusion(f32[2,16,96,128]{2,1,3,0:T(8,128)S(1)} %get-tuple-element.17, f32[2,16,96,2]{2,1,3,0:T(8,128)S(1)} %collective-permute-done.3, f32[2,16,96,128]{2,1,3,0:T(8,128)} %copy-done.5, f32[2,16,96,2]{2,1,3,0:T(8,128)S(1)} %collective-permute-done.2, f32[2,16,96,128]{2,1,3,0:T(8,128)S(1)} %get-tuple-element.8, ...), kind=kLoop, calls=%fused_computation.140 | loop fusion | flops 12582912 | bytes 7127040 | tf_op jit(solution)/shard_map/sub | solution.py:79
  753.9 0.8 fusion.167
  754.7 1.7 collective-permute-start.5
  756.4 13.6 %fusion.28 = f32[2,16,96,128]{2,1,3,0:T(8,128)S(1)} fusion(f32[2,16,96,128]{2,1,3,0:T(8,128)S(1)} %get-tuple-element.18, f32[2,16,96,2]{2,1,3,0:T(8,128)S(1)} %collective-permute-done.9, f32[2,16,96,128]{2,1,3,0:T(8,128)} %get-tuple-element.9, f32[2,16,96,2]{2,1,3,0:T(8,128)S(1)} %collective-permute-done.8, f32[2,16,96,128]{2,1,3,0:T(8,128)S(1)} %get-tuple-element.10, ...), kind=kLoop, calls=%fused_computation.100 | loop fusion | flops 12582912 | bytes 7127040 | tf_op jit(solution)/shard_map/sub | solution.py:79
  770.0 1.4 copy-done.4
  771.4 0.6 fusion.170
  772.0 1.7 collective-permute-start.11
  773.7 2.4 broadcast_multiply_fusion.5
  776.1 2.5 copy.10
  778.6 2.5 copy.5
  781.2 26.4 %fusion.15 = f32[2,16,96,128]{2,1,3,0:T(8,128)} fusion(f32[2,16,96,2]{2,1,3,0:T(8,128)S(1)} %collective-permute-done.11, f32[2,16,96,128]{2,1,3,0:T(8,128)} %copy-done.4, f32[2,16,96,2]{2,1,3,0:T(8,128)S(1)} %collective-permute-done.10, f32[2,16,96,2]{2,1,3,0:T(8,128)S(1)} %collective-permute-done.5, f32[2,16,96,128]{2,1,3,0:T(8,128)} %fusion.68, ...), kind=kLoop, calls=%fused_computation.87 | loop fusion | flops 32636928 | bytes 13467648 | tf_op jit(solution)/shard_map/add | solution.py:84
  807.6 2.9 copy.13
  (37 shorter events, 0.2 us)
Async XLA Ops:
  6.5 661.7 %all-reduce.9.cloned.1.call-start = ((), (), s32[]{:S(2)}) async-start(), calls=%async_computation | async-start | bytes 3145728 | tf_op jit(solution)/shard_map/psum | solution.py:34
  11.5 3.0 copy-start.6
  668.3 2.6 copy-start.8
  674.7 81.7 %copy-start = (f32[2,16,96,128]{2,1,3,0:T(8,128)}, f32[2,16,96,128]{2,1,3,0:T(8,128)S(1)}, u32[]{:S(2)}) copy-start(f32[2,16,96,128]{2,1,3,0:T(8,128)S(1)} %get-tuple-element.18) | copy-start | bytes 4718596
  674.7 49.2 %collective-permute-start = (f32[2,16,96,2]{2,1,3,0:T(8,128)S(1)}, f32[2,16,96,2]{2,1,3,0:T(8,128)S(1)}, u32[]{:S(2)}, u32[]{:S(2)}) collective-permute-start(f32[2,16,96,2]{2,1,3,0:T(8,128)S(1)} %get-tuple-element.15), channel_id=1, source_target_pairs={{1,0},{2,1},{3,2},{0,3},{5,4},{6,5},{7,6},{4,7},{9,8},{10,9},{11,1... | collective-permute-start | bytes 73736 | tf_op jit(solution)/shard_map/ppermute | solution.py:27
  721.9 2.0 collective-permute-start.1
  722.2 8.6 %collective-permute-start.6 = (f32[2,16,96,2]{2,1,3,0:T(8,128)S(1)}, f32[2,16,96,2]{2,1,3,0:T(8,128)S(1)}, u32[]{:S(2)}, u32[]{:S(2)}) collective-permute-start(f32[2,16,96,2]{2,1,3,0:T(8,128)S(1)} %get-tuple-element.23), channel_id=1, source_target_pairs={{1,0},{2,1},{3,2},{0,3},{5,4},{6,5},{7,6},{4,7},{9,8},{10,9},{11,1... | collective-permute-start | bytes 73736 | tf_op jit(solution)/shard_map/ppermute | solution.py:27
  722.5 8.3 %collective-permute-start.7 = (f32[2,16,96,2]{2,1,3,0:T(8,128)S(1)}, f32[2,16,96,2]{2,1,3,0:T(8,128)S(1)}, u32[]{:S(2)}, u32[]{:S(2)}) collective-permute-start(f32[2,16,96,2]{2,1,3,0:T(8,128)S(1)} %get-tuple-element.24), channel_id=1, source_target_pairs={{0,1},{1,2},{2,3},{3,0},{4,5},{5,6},{6,7},{7,4},{8,9},{9,10},{10,1... | collective-permute-start | bytes 73736 | tf_op jit(solution)/shard_map/ppermute | solution.py:26
  728.7 2.1 copy-start.5
  728.7 10.3 %copy-start.1 = (f32[2,16,96,128]{2,1,3,0:T(8,128)}, f32[2,16,96,128]{2,1,3,0:T(8,128)S(1)}, u32[]{:S(2)}) copy-start(f32[2,16,96,128]{2,1,3,0:T(8,128)S(1)} %get-tuple-element.8) | copy-start | bytes 4718596
  728.7 10.3 %collective-permute-start.2 = (f32[2,16,96,2]{2,1,3,0:T(8,128)S(1)}, f32[2,16,96,2]{2,1,3,0:T(8,128)S(1)}, u32[]{:S(2)}, u32[]{:S(2)}) collective-permute-start(f32[2,16,96,2]{2,1,3,0:T(8,128)S(1)} %get-tuple-element.13), channel_id=1, source_target_pairs={{1,0},{2,1},{3,2},{0,3},{5,4},{6,5},{7,6},{4,7},{9,8},{10,9},{11,1... | collective-permute-start | bytes 73736 | tf_op jit(solution)/shard_map/ppermute | solution.py:27
  730.2 8.8 %copy-start.3 = (f32[16,96,128]{1,0,2:T(8,128)S(1)}, f32[16,96,128]{1,0,2:T(8,128)}, u32[]{:S(2)}) copy-start(f32[16,96,128]{1,0,2:T(8,128)} %copy.9) | copy-start | bytes 2359300
  730.2 8.8 %collective-permute-start.3 = (f32[2,16,96,2]{2,1,3,0:T(8,128)S(1)}, f32[2,16,96,2]{2,1,3,0:T(8,128)S(1)}, u32[]{:S(2)}, u32[]{:S(2)}) collective-permute-start(f32[2,16,96,2]{2,1,3,0:T(8,128)S(1)} %get-tuple-element.14), channel_id=1, source_target_pairs={{0,1},{1,2},{2,3},{3,0},{4,5},{5,6},{6,7},{7,4},{8,9},{9,10},{10,1... | collective-permute-start | bytes 73736 | tf_op jit(solution)/shard_map/ppermute | solution.py:26
  736.4 20.0 %copy-start.2 = (f32[2,16,96,128]{2,1,3,0:T(8,128)}, f32[2,16,96,128]{2,1,3,0:T(8,128)S(1)}, u32[]{:S(2)}) copy-start(f32[2,16,96,128]{2,1,3,0:T(8,128)S(1)} %get-tuple-element.10) | copy-start | bytes 4718596
  737.3 19.1 %collective-permute-start.8 = (f32[2,16,96,2]{2,1,3,0:T(8,128)S(1)}, f32[2,16,96,2]{2,1,3,0:T(8,128)S(1)}, u32[]{:S(2)}, u32[]{:S(2)}) collective-permute-start(f32[2,16,96,2]{2,1,3,0:T(8,128)S(1)} %get-tuple-element.21), channel_id=1, source_target_pairs={{1,0},{2,1},{3,2},{0,3},{5,4},{6,5},{7,6},{4,7},{9,8},{10,9},{11,1... | collective-permute-start | bytes 73736 | tf_op jit(solution)/shard_map/ppermute | solution.py:27
  737.9 18.5 %collective-permute-start.9 = (f32[2,16,96,2]{2,1,3,0:T(8,128)S(1)}, f32[2,16,96,2]{2,1,3,0:T(8,128)S(1)}, u32[]{:S(2)}, u32[]{:S(2)}) collective-permute-start(f32[2,16,96,2]{2,1,3,0:T(8,128)S(1)} %get-tuple-element.22), channel_id=1, source_target_pairs={{0,1},{1,2},{2,3},{3,0},{4,5},{5,6},{6,7},{7,4},{8,9},{9,10},{10,1... | collective-permute-start | bytes 73736 | tf_op jit(solution)/shard_map/ppermute | solution.py:26
  754.6 26.5 %collective-permute-start.4 = (f32[2,16,96,2]{2,1,3,0:T(8,128)S(1)}, f32[2,16,96,2]{2,1,3,0:T(8,128)S(1)}, u32[]{:S(2)}, u32[]{:S(2)}) collective-permute-start(f32[2,16,96,2]{2,1,3,0:T(8,128)S(1)} %get-tuple-element.11), channel_id=1, source_target_pairs={{1,0},{2,1},{3,2},{0,3},{5,4},{6,5},{7,6},{4,7},{9,8},{10,9},{11,1... | collective-permute-start | bytes 73736 | tf_op jit(solution)/shard_map/ppermute | solution.py:27
  754.7 26.5 %collective-permute-start.5 = (f32[2,16,96,2]{2,1,3,0:T(8,128)S(1)}, f32[2,16,96,2]{2,1,3,0:T(8,128)S(1)}, u32[]{:S(2)}, u32[]{:S(2)}) collective-permute-start(f32[2,16,96,2]{2,1,3,0:T(8,128)S(1)} %get-tuple-element.12), channel_id=1, source_target_pairs={{0,1},{1,2},{2,3},{3,0},{4,5},{5,6},{6,7},{7,4},{8,9},{9,10},{10,1... | collective-permute-start | bytes 73736 | tf_op jit(solution)/shard_map/ppermute | solution.py:26
  756.4 17.3 %copy-start.7 = (f32[16,96,128]{2,1,0:T(8,128)S(1)}, f32[16,96,128]{2,1,0:T(8,128)}, u32[]{:S(2)}) copy-start(f32[16,96,128]{2,1,0:T(8,128)} %get-tuple-element.5) | copy-start | bytes 2359300
  770.0 1.4 copy-start.4
  772.0 9.2 %collective-permute-start.10 = (f32[2,16,96,2]{2,1,3,0:T(8,128)}, f32[2,16,96,2]{2,1,3,0:T(8,128)S(1)}, u32[]{:S(2)}, u32[]{:S(2)}) collective-permute-start(f32[2,16,96,2]{2,1,3,0:T(8,128)} %get-tuple-element.19), channel_id=1, source_target_pairs={{1,0},{2,1},{3,2},{0,3},{5,4},{6,5},{7,6},{4,7},{9,8},{10,9},{11,1... | collective-permute-start | bytes 73736 | tf_op jit(solution)/shard_map/ppermute | solution.py:27
  772.0 9.2 %collective-permute-start.11 = (f32[2,16,96,2]{2,1,3,0:T(8,128)}, f32[2,16,96,2]{2,1,3,0:T(8,128)S(1)}, u32[]{:S(2)}, u32[]{:S(2)}) collective-permute-start(f32[2,16,96,2]{2,1,3,0:T(8,128)} %get-tuple-element.20), channel_id=1, source_target_pairs={{0,1},{1,2},{2,3},{3,0},{4,5},{5,6},{6,7},{7,4},{8,9},{9,10},{10,1... | collective-permute-start | bytes 73736 | tf_op jit(solution)/shard_map/ppermute | solution.py:26
Sparse Core Ops, SparseCore 0:
  11.7 656.5 all-reduce.8
where the time goes:
time: 818 us; the launch traced here: 817 us
  waiting for transfers between devices  652 us (80%)
  other arithmetic  72.6 us (9%)
  starting transfers between devices  56.5 us (7%)
  local copies, waits for them, and re-layouts  21.7 us (3%)
  between operations  14.8 us (2%)
    psum x1, waiting for transfers between devices, broadcast(): return lax.psum(block, axis)  652 us
    ppermute x6, starting transfers between devices, with_halo(): after = lax.ppermute(leading, axis, down)  49.7 us
    sub x2, other arithmetic, body(): third = 2.0 * scaled_step(second, potential) - first  28.4 us
    add x1, other arithmetic, body(): total = total + occupation * orbital[None] * filtered  26.4 us
  transfers between devices with their start and end apart: 13, of which 1 were waited for; matrix products, arithmetic and copies ran while one was open for 7% of the time, Pallas kernels for 0%

commit v1 on v0

v1 whole, which is shorter than its diff:
```python
import functools

import jax
import jax.numpy as jnp
from jax import lax
from jax.experimental import pallas as pl
from jax.experimental.pallas import tpu as pltpu
from jax.sharding import PartitionSpec as P

MESH = pl.DeviceIdType.MESH
F32 = jnp.float32

ROUNDS = 2
X, Z, H = 4, 8, 2
PAD = 16
HALO = 8


def coords(index):
    return index // (Z * H), (index // H) % Z, index % H


def at(x, z, h):
    return (x * Z + z) * H + h


def pick(select, yes, no):
    return jnp.where(jnp.full(yes.shape, select, jnp.int32) != 0, yes, no)


class Ring:
    def __init__(self, name, me):
        x, z, h = me
        self.name = name
        self.size = {"x": X, "z": Z}[name]
        self.me = {"x": x, "z": z}[name]

        def move(step):
            if name == "x":
                return at((x + step + X) % X, z, h)
            return at(x, (z + step + Z) % Z, h)

        self.right, self.left = move(1), move(-1)


class Sems:
    def __init__(self, send, recv):
        self.send, self.recv, self.count = send, recv, 0

    def take(self):
        self.count += 1
        return self.send.at[self.count - 1], self.recv.at[self.count - 1]


def remote(src, dst, sems, cols, sec):
    send, recv = sems.take()
    return pltpu.make_async_remote_copy(
        src_ref=src, dst_ref=dst, send_sem=send, recv_sem=recv, device_id=(cols, sec), device_id_type=MESH
    )


def rows(ref, start, size):
    return ref.at[pl.ds(pl.multiple_of(start, 8), size), :]


def spread(own, base, size, out, slots, first, second, me, root, flip, sems, sent):
    sec = lax.axis_index("sec")
    x, z, h = me
    taken = [0]

    def slot(n):
        taken[0] += n
        return slots.at[pl.ds(taken[0] - n, n), :]

    def go(src, dst, cols):
        copy = remote(src, dst, sems, cols, sec)
        copy.start()
        sent.append(copy)
        return copy

    def counts(ring):
        more, fewer = ring.size // 2, (ring.size - 1) // 2
        return (fewer, more) if flip else (more, fewer)

    def scatter(src, offset, piece, ring, root_at):
        n, i = ring.size, ring.me
        n_right, n_left = counts(ring)
        mine = jnp.where(root_at == i, 1, 0)
        right = left = None
        for step in range(1, max(n_right, n_left) + 1):
            for way, last, target in ((1, n_right, ring.right), (-1, n_left, ring.left)):
                if step > last:
                    continue
                held = right if way == 1 else left
                which = (i + way * (last + 1 - step) + n) % n
                source = rows(src, offset + which * piece, piece)
                if step > 1:
                    held[1].wait_recv()
                    merged = slot(piece)
                    merged[...] = pick(mine, source[...], held[0][...])
                    source = merged
                landing = slot(piece)
                copy = go(source, landing, target)
                if way == 1:
                    right = (landing, copy)
                else:
                    left = (landing, copy)
            yield None
        value = rows(src, offset + i * piece, piece)[...]
        behind = (i - root_at + n) % n
        if right is not None:
            right[1].wait_recv()
            value = pick(jnp.where((behind >= 1) & (behind <= n_right), 1, 0), right[0][...], value)
        if left is not None:
            left[1].wait_recv()
            value = pick(jnp.where(behind > n_right, 1, 0), left[0][...], value)
        yield value

    def gather(offset, piece, ring):
        n, i = ring.size, ring.me
        n_right, n_left = counts(ring)
        copies = {}
        for step in range(1, max(n_right, n_left) + 1):
            for way, last, target in ((1, n_right, ring.right), (-1, n_left, ring.left)):
                if step > last:
                    continue
                if step > 1:
                    copies[way].wait_recv()
                which = (i - way * (step - 1) + n) % n
                place = rows(out, offset + which * piece, piece)
                copies[way] = go(place, place, target)
            yield
        for copy in copies.values():
            copy.wait_recv()

    piece1 = size // first.size
    piece2 = piece1 // second.size
    root_x, root_z, root_h = root
    root1, root2 = (root_z, root_x) if first.name == "z" else (root_x, root_z)

    value = None
    for value in scatter(own, base, piece1, first, root1):
        if value is None:
            yield
    held = slot(piece1)
    held[...] = value
    for value in scatter(held, 0, piece2, second, root2):
        if value is None:
            yield
    place = base + first.me * piece1 + second.me * piece2
    final = rows(out, place, piece2)
    if H > 1:
        mid, landing = slot(piece2), slot(piece2)
        mid[...] = value
        copy = go(mid, landing, at(x, z, (h + 1) % H))
        yield
        copy.wait_recv()
        value = pick(jnp.where(root_h == h, 1, 0), value, landing[...])
    final[...] = value
    yield from gather(base + first.me * piece1, piece2, second)
    yield from gather(base, piece1, first)


def slot_rows(size):
    def one(n, piece):
        return (2 * (n - 1)) * piece

    a = one(Z, size // Z) + size // Z + one(X, size // (Z * X)) + 2 * size // (Z * X)
    b = one(X, size // X) + size // X + one(Z, size // (Z * X)) + 2 * size // (Z * X)
    return max(a, b)


def turned(plane, nz):
    return jnp.concatenate([plane, jnp.zeros((128 - nz, 128), F32)], axis=0).T


def stencil(src, d_ref, y, ny, row):
    def read(plane, shift):
        return src[plane, pl.ds(row + shift, 8), :]

    u = read(y, 0)
    near = read(y, 1) + read(y, -1)
    far = read(y, 2) + read(y, -2)
    near = near + (pltpu.roll(u, 1, 1) + pltpu.roll(u, 127, 1))
    far = far + (pltpu.roll(u, 2, 1) + pltpu.roll(u, 126, 1))
    for shift in (-1, 1):
        if 0 <= y + shift < ny:
            near = near + read(y + shift, 0)
    for shift in (-2, 2):
        if 0 <= y + shift < ny:
            far = far + read(y + shift, 0)
    return (far - 16.0 * near) + d_ref[y, pl.ds(row, 8), :] * u


def kernel(
    owner_ref, trial_ref, orbital_ref, potential_ref, out_ref,
    trial_v, orbital_v, potential_v, psi, slots, psi_t, trial_t, d_t, w, u1, u2, total, out_v,
    load_sem, store_sem, send_sem, recv_sem,
):
    ny, nz, nx = potential_v.shape
    n_rows = ny * nz
    sec = lax.axis_index("sec")
    n_sec = lax.axis_size("sec")
    cols = lax.axis_index("cols")
    me = coords(cols)
    x, z, h = me
    ring_x, ring_z = Ring("x", me), Ring("z", me)
    sec_right, sec_left = (sec + 1) % n_sec, (sec + n_sec - 1) % n_sec

    loads = [
        pltpu.make_async_copy(orbital_ref.at[0], orbital_v, load_sem.at[0]),
        pltpu.make_async_copy(trial_ref, trial_v, load_sem.at[1]),
        pltpu.make_async_copy(potential_ref, potential_v, load_sem.at[2]),
    ]
    for load in loads:
        load.start()

    barrier = pltpu.get_barrier_semaphore()
    partners = [(ring_x.right, sec), (ring_x.left, sec), (ring_z.right, sec), (ring_z.left, sec)]
    if H > 1:
        partners.append((at(x, z, (h + 1) % H), sec))
    partners += [(cols, sec_right), (cols, sec_left)]
    for partner in partners:
        pl.semaphore_signal(barrier, inc=1, device_id=partner, device_id_type=MESH)
    pl.semaphore_wait(barrier, len(partners))

    sems = Sems(send_sem, recv_sem)
    sent = []
    loads[0].wait()

    half = n_rows // 2
    parts = []
    for turn in range(ROUNDS):
        root = coords(owner_ref[turn])
        for part, (first, second) in enumerate(((ring_z, ring_x), (ring_x, ring_z))):
            parts.append(
                spread(
                    orbital_v, part * half, half, psi.at[turn], slots.at[2 * turn + part],
                    first, second, me, root, turn == 1, sems, sent,
                )
            )

    def advance(which):
        for part in which:
            next(part, None)

    def swap_edges(ref, lead):
        every = (slice(None),) * lead
        first = ref.at[every + (pl.ds(PAD, HALO),)]
        last = ref.at[every + (pl.ds(PAD + nx - HALO, HALO),)]
        before = ref.at[every + (pl.ds(PAD - HALO, HALO),)]
        after = ref.at[every + (pl.ds(PAD + nx, HALO),)]
        copies = [
            remote(last, before, sems, cols, sec_right),
            remote(first, after, sems, cols, sec_left),
        ]
        for copy in copies:
            copy.start()
            sent.append(copy)
        return copies

    def turn_all(read, write):
        def one(y, carry):
            write(y, turned(read(y), nz))
            return carry

        lax.fori_loop(0, ny, one, 0)

    advance(parts)
    loads[2].wait()

    def put_d(y, value):
        d_t[y, PAD : PAD + nx, :] = 6.0 * (value - 1.0)

    turn_all(lambda y: potential_v[y], put_d)
    edges_d = swap_edges(d_t, 1)
    advance(parts)
    loads[1].wait()
    for column in range(2):
        def put_trial(y, value, column=column):
            trial_t[column, y, PAD : PAD + nx, :] = value

        turn_all(lambda y, column=column: trial_v[column, y], put_trial)
        advance(parts)
    edges_trial = swap_edges(trial_t, 2)
    for _ in range(64):
        advance(parts)
    for copy in edges_d + edges_trial:
        copy.wait_recv()

    lanes = lax.broadcasted_iota(jnp.int32, (8, 128), 1)
    inside = lanes < nz

    def field_rows(turn, column, lo, hi):
        def one(block, carry):
            row = pl.multiple_of(block * 8, 8)
            for y in range(ny):
                w[column, y, pl.ds(row, 8), :] = (
                    psi_t[turn, y, pl.ds(row, 8), :] * trial_t[column, y, pl.ds(row, 8), :]
                )
            return carry

        lax.fori_loop(lo, hi, one, 0)

    def step_rows(src, dst, column, scale, sign, lo, hi):
        def one(block, carry):
            row = pl.multiple_of(block * 8, 8)
            for y in range(ny):
                v = stencil(src.at[column], d_t, y, ny, row)
                value = scale * w[column, y, pl.ds(row, 8), :] + sign * v
                dst[column, y, pl.ds(row, 8), :] = jnp.where(inside, value, 0.0)
            return carry

        lax.fori_loop(lo, hi, one, 0)

    def last_rows(turn, column, lo, hi):
        def one(block, carry):
            row = pl.multiple_of(block * 8, 8)
            place = pl.multiple_of(row - PAD, 8)
            for y in range(ny):
                v = stencil(u2.at[column], d_t, y, ny, row)
                value = psi_t[turn, y, pl.ds(row, 8), :] * (
                    0.2 * w[column, y, pl.ds(row, 8), :] + v * (1.0 / 864000.0)
                )
                if turn > 0:
                    value = value + total[column, y, pl.ds(place, 8), :]
                total[column, y, pl.ds(place, 8), :] = value
            return carry

        lax.fori_loop(lo, hi, one, 0)

    a, b = PAD // 8, (PAD + nx) // 8
    for turn in range(ROUNDS):
        def put_psi(y, value, turn=turn):
            psi_t[turn, y, PAD : PAD + nx, :] = value

        def get_psi(y, turn=turn):
            return psi[turn, pl.ds(pl.multiple_of(y * nz, 8), nz), :]

        turn_all(get_psi, put_psi)
        edges = swap_edges(psi_t.at[turn], 1)
        for column in range(2):
            field_rows(turn, column, a, b)
            step_rows(w, u1, column, 72.0, -1.0, a + 1, b - 1)
        for copy in edges:
            copy.wait_recv()
        for column in range(2):
            field_rows(turn, column, a - 1, a)
            field_rows(turn, column, b, b + 1)
            step_rows(w, u1, column, 72.0, -1.0, a - 1, a + 1)
            step_rows(w, u1, column, 72.0, -1.0, b - 1, b + 1)
            step_rows(u1, u2, column, 3600.0, 1.0, a - 1, b + 1)
            last_rows(turn, column, a, b)

    stores = []
    for column in range(2):
        def back(y, carry, column=column):
            out_v[column, y] = total[column, y].T[:nz, :]
            return carry

        lax.fori_loop(0, ny, back, 0)
        store = pltpu.make_async_copy(out_v.at[column], out_ref.at[column], store_sem.at[column])
        store.start()
        stores.append(store)
    for copy in sent:
        copy.wait_send()
    for store in stores:
        store.wait()


def body(trial, orbitals, potential, owner):
    columns, ny, nz, nx = trial.shape
    n_rows = ny * nz
    tall = PAD + nx + PAD
    any_spec = pl.BlockSpec(memory_space=pl.ANY)
    n_sems = 2 * ROUNDS * (2 * (X - 1) + 2 * (Z - 1) + 1) + 2 * (2 + ROUNDS)
    return pl.pallas_call(
        kernel,
        out_shape=jax.ShapeDtypeStruct(trial.shape, F32),
        in_specs=[pl.BlockSpec(memory_space=pltpu.SMEM), any_spec, any_spec, any_spec],
        out_specs=any_spec,
        scratch_shapes=[
            pltpu.VMEM(trial.shape, F32),
            pltpu.VMEM((n_rows, nx), F32),
            pltpu.VMEM((ny, nz, nx), F32),
            pltpu.VMEM((ROUNDS, n_rows, nx), F32),
            pltpu.VMEM((2 * ROUNDS, slot_rows(n_rows // 2), nx), F32),
            pltpu.VMEM((ROUNDS, ny, tall, 128), F32),
            pltpu.VMEM((columns, ny, tall, 128), F32),
            pltpu.VMEM((ny, tall, 128), F32),
            pltpu.VMEM((columns, ny, tall, 128), F32),
            pltpu.VMEM((columns, ny, tall, 128), F32),
            pltpu.VMEM((columns, ny, tall, 128), F32),
            pltpu.VMEM((columns, ny, nx, 128), F32),
            pltpu.VMEM(trial.shape, F32),
            pltpu.SemaphoreType.DMA((3,)),
            pltpu.SemaphoreType.DMA((columns,)),
            pltpu.SemaphoreType.DMA((n_sems,)),
            pltpu.SemaphoreType.DMA((n_sems,)),
        ],
        compiler_params=pltpu.CompilerParams(
            collective_id=0, has_side_effects=True, vmem_limit_bytes=52 * 1024 * 1024
        ),
    )(owner, trial, orbitals.reshape(orbitals.shape[0], n_rows, nx), potential)


def solution(mesh):
    placed = (P("cols", None, None, "sec"), P("cols", None, None, "sec"), P(None, None, "sec"), P())
    return jax.shard_map(
        body, mesh=mesh, in_specs=placed, out_specs=P("cols", None, None, "sec"), check_vma=False
    )
```

time: 818 us -> 99.5 us (0.12)
  waiting for transfers between devices: 652 us -> 0 us
  Pallas kernels: 0 us -> 93.4 us
  other arithmetic: 72.6 us -> 0 us
  starting transfers between devices: 56.5 us -> 0 us
  local copies, waits for them, and re-layouts: 21.7 us -> 5.58 us
  between operations: 14.8 us -> 0.01 us
    psum x1 -> x0, waiting for transfers between devices: 652 us -> none  [broadcast(): return lax.psum(block, axis)]
    pallas_call x0 -> x1, Pallas kernels: none -> 93.4 us  [body(): pl.pallas_call(kernel, out_shape=jax.ShapeDtypeStruct(trial.shape, F32),...]
    ppermute x12 -> x0, starting transfers between devices: 56.5 us -> none  [the longest x6 49.7 us: with_halo(): after = lax.ppermute(leading, axis, down)]
    sub x2 -> x0, other arithmetic: 28.4 us -> none  [body(): third = 2.0 * scaled_step(second, potential) - first]
    add x1 -> x0, other arithmetic: 26.4 us -> none  [body(): total = total + occupation * orbital[None] * filtered]
    div x2 -> x0, other arithmetic: 10.4 us -> none  [apply_scaled(): (kinetic + potential * center - spectrum_mid * center) / spectrum_half]
  transfers between devices with their start and end apart: 13 -> 0, of which waited for: 1 -> 0; matrix products, arithmetic and copies ran while one was open for 7% -> 0% of each run, Pallas kernels for 0% -> 0%
where the time goes in v1:
time: 99.5 us; the launch traced here: 99 us
  Pallas kernels  93.4 us (94%)
  local copies, waits for them, and re-layouts  5.58 us (6%)
    pallas_call x1, Pallas kernels, body(): pl.pallas_call(kernel, out_shape=jax.ShapeDtypeStruct(trial.shape, F32),...  93.4 us
    unnamed x7, local copies, waits for them, and re-layouts  5.58 us

profile of v1, /device:TPU:1, one launch (start us, length us, event | category | flops | bytes accessed | tf_op | source)
XLA Modules:
  0.0 99.0 jit_solution(1002808216258921221)
XLA Ops:
  0.0 0.0 copy-start
  0.0 1.1 %copy-done = f32[1,16,96,128]{3,2,1,0:T(8,128)S(1)} copy-done((f32[1,16,96,128]{3,2,1,0:T(8,128)S(1)}, f32[1,16,96,128]{3,2,1,0:T(8,128)}, u32[]{:S(2)}) %copy-start) | copy-done | bytes 786456
  1.1 0.0 copy-start.1
  1.1 1.1 %copy-done.1 = f32[16,96,128]{2,1,0:T(8,128)S(1)} copy-done((f32[16,96,128]{2,1,0:T(8,128)S(1)}, f32[16,96,128]{2,1,0:T(8,128)}, u32[]{:S(2)}) %copy-start.1) | copy-done | bytes 786456
  2.3 0.0 copy-start.2
  2.3 0.7 copy-done.2
  2.9 93.4 %shard_map.46 = f32[2,16,96,128]{3,2,1,0:T(8,128)} custom-call(s32[2]{0:T(128)S(1)} %copy-done.2, f32[2,16,96,128]{3,2,1,0:T(8,128)} %trial_ref.1, f32[1,1536,128]{2,1,0:T(8,128)S(1)} %bitcast.1, f32[16,96,128]{2,1,0:T(8,128)S(1)} %copy-done.1), custom_call_target="tpu_custom_call" | custom-call | tf_op jit(solution)/shard_map/pallas_call | solution.py:377
  96.3 2.7 %copy.6 = f32[2,16,96,128]{3,2,1,0:T(8,128)} copy(f32[2,16,96,128]{3,2,1,0:T(8,128)} %shard_map.46) | data formatting | bytes 3145728
Async XLA Ops:
  0.0 1.1 %copy-start = (f32[1,16,96,128]{3,2,1,0:T(8,128)S(1)}, f32[1,16,96,128]{3,2,1,0:T(8,128)}, u32[]{:S(2)}) copy-start(f32[1,16,96,128]{3,2,1,0:T(8,128)} %param.5) | copy-start | bytes 2359300
  1.1 1.1 %copy-start.1 = (f32[16,96,128]{2,1,0:T(8,128)S(1)}, f32[16,96,128]{2,1,0:T(8,128)}, u32[]{:S(2)}) copy-start(f32[16,96,128]{2,1,0:T(8,128)} %potential_ref.1) | copy-start | bytes 2359300
  2.3 0.7 copy-start.2

commit v2 on v0

v2 whole, which is shorter than its diff:
```python
import jax
import jax.numpy as jnp
from jax import lax
from jax.experimental import pallas as pl
from jax.experimental.pallas import tpu as pltpu
from jax.sharding import PartitionSpec as P

MESH = pl.DeviceIdType.MESH
F32 = jnp.float32

ROUNDS = 2
X, Z, H = 4, 8, 2
PAD = 16
BLOCK = 16
TOGETHER = ((0, 1),)
HALO = 8


def coords(index):
    return index // (Z * H), (index // H) % Z, index % H


def at(x, z, h):
    return (x * Z + z) * H + h


class Group:
    def __init__(self, name, me):
        self.name, self.me = name, me
        self.size = Z if name == "z" else X * H

    def shifted(self, offset):
        x, z, h = self.me
        if self.name == "z":
            return x, (z + offset) % Z, h
        return (x + offset // H) % X, z, (h + offset % H) % H

    def member(self, offset):
        return at(*self.shifted(offset))

    def place(self, offset=0):
        x, z, h = self.shifted(offset)
        return z if self.name == "z" else x * H + h

    def offset_of(self, root):
        x, z, h = self.me
        rx, rz, rh = root
        if self.name == "z":
            return (z - rz + Z) % Z
        return ((x - rx + X) % X) * H + (h - rh + H) % H


class Sems:
    def __init__(self, send, recv):
        self.send, self.recv, self.count = send, recv, 0

    def take(self):
        self.count += 1
        return self.send.at[self.count - 1], self.recv.at[self.count - 1]


def remote(src, dst, sems, cols, sec):
    send, recv = sems.take()
    return pltpu.make_async_remote_copy(
        src_ref=src, dst_ref=dst, send_sem=send, recv_sem=recv, device_id=(cols, sec), device_id_type=MESH
    )


def rows(ref, start, size):
    return ref.at[pl.ds(pl.multiple_of(start, 8), size), :]


def spread(first_copy, own, base, size, out, landed1, landed2, held, first, second, root, sems, sent):
    sec = lax.axis_index("sec")

    def go(src, dst, cols):
        copy = remote(src, dst, sems, cols, sec)
        copy.start()
        sent.append(copy)
        return copy

    def scatter(src, offset, piece, group, landed):
        return [
            go(rows(src, offset + group.place(k) * piece, piece), landed.at[k], group.member(k))
            for k in range(1, group.size)
        ]

    def taken(copies, src, offset, piece, group, landed):
        landed[0] = rows(src, offset + group.place() * piece, piece)[...]
        for copy in copies:
            copy.wait_recv()
        return landed[group.offset_of(root)]

    def gather(offset, piece, group):
        place = rows(out, offset + group.place() * piece, piece)
        return [go(place, place, group.member(k)) for k in range(1, group.size)]

    piece1 = size // first.size
    piece2 = piece1 // second.size
    inner = base + first.place() * piece1
    copies = scatter(first_copy, base, piece1, first, landed1)
    yield
    held[...] = taken(copies, own, base, piece1, first, landed1)
    copies = scatter(held, 0, piece2, second, landed2)
    yield
    rows(out, inner + second.place() * piece2, piece2)[...] = taken(copies, held, 0, piece2, second, landed2)
    copies = gather(inner, piece2, second)
    yield
    for copy in copies:
        copy.wait_recv()
    copies = gather(base, piece1, first)
    yield
    for copy in copies:
        copy.wait_recv()


def turned(plane, nz):
    return jnp.concatenate([plane, jnp.zeros((128 - nz, 128), F32)], axis=0).T


def along_lanes(fields, band):
    height = fields[0].shape[0]
    whole = jnp.concatenate(fields, axis=0)
    high = whole.astype(jnp.bfloat16)
    low = (whole - high.astype(F32)).astype(jnp.bfloat16)
    both = jnp.concatenate([high, low], axis=1)
    product = jnp.dot(both, band, preferred_element_type=F32)
    return [product[height * i : height * (i + 1), :] for i in range(len(fields))]


def stencil(src, d_ref, band, columns, ny, row, store):
    def read(column, plane, shift):
        return src[column, plane, pl.ds(row + shift, BLOCK), :]

    u = {(c, y): read(c, y, 0) for c in columns for y in range(ny)}
    lanes = dict(zip(u, along_lanes(list(u.values()), band)))
    for c, y in u:
        near = read(c, y, 1) + read(c, y, -1)
        far = read(c, y, 2) + read(c, y, -2)
        for shift in (-1, 1):
            if 0 <= y + shift < ny:
                near = near + u[c, y + shift]
        for shift in (-2, 2):
            if 0 <= y + shift < ny:
                far = far + u[c, y + shift]
        store(c, y, (far - 16.0 * near) + (lanes[c, y] + d_ref[y, pl.ds(row, BLOCK), :] * u[c, y]))


def kernel(
    owner_ref, trial_ref, orbital_ref, potential_ref, out_ref,
    trial_v, orbital_v, potential_v, psi, land_p1, land_p2, land_q1, land_q2, held_p, held_q,
    psi_t, trial_t, d_t, w, u1, u2, total, band_ref,
    load_sem, store_sem, send_sem, recv_sem,
):
    ny, nz, nx = potential_v.shape
    n_rows = ny * nz
    sec = lax.axis_index("sec")
    n_sec = lax.axis_size("sec")
    cols = lax.axis_index("cols")
    me = coords(cols)
    group_xy, group_z = Group("xy", me), Group("z", me)
    sec_right, sec_left = (sec + 1) % n_sec, (sec + n_sec - 1) % n_sec

    barrier = pltpu.get_barrier_semaphore()
    partners = [(g.member(k), sec) for g in (group_xy, group_z) for k in range(1, g.size)]
    partners += [(cols, sec_right), (cols, sec_left)]
    for partner in partners:
        pl.semaphore_signal(barrier, inc=1, device_id=partner, device_id_type=MESH)

    loads = [
        pltpu.make_async_copy(orbital_ref.at[0], orbital_v, load_sem.at[0]),
        pltpu.make_async_copy(potential_ref, potential_v, load_sem.at[1]),
        pltpu.make_async_copy(trial_ref, trial_v, load_sem.at[2]),
    ]
    for load in loads:
        load.start()

    k = lax.broadcasted_iota(jnp.int32, (256, 128), 0) % 128
    n = lax.broadcasted_iota(jnp.int32, (256, 128), 1)
    gap = jnp.abs(k - n)
    weight = jnp.where(gap == 1, -16.0, jnp.where(gap == 2, 1.0, 0.0))
    band_ref[...] = jnp.where((k < nz) & (n < nz), weight, 0.0).astype(jnp.bfloat16)

    pl.semaphore_wait(barrier, len(partners))

    sems = Sems(send_sem, recv_sem)
    sent = []
    size_p = 2 * n_rows // 3
    parts = []
    for turn in range(ROUNDS):
        root = coords(owner_ref[turn])
        parts.append(
            spread(
                orbital_ref.at[0], orbital_v, 0, size_p, psi[turn], land_p1[turn], land_p2[turn],
                held_p[turn], group_xy, group_z, root, sems, sent,
            )
        )
        parts.append(
            spread(
                orbital_ref.at[0], orbital_v, size_p, n_rows - size_p, psi[turn], land_q1[turn],
                land_q2[turn], held_q[turn], group_z, group_xy, root, sems, sent,
            )
        )

    def advance(which):
        for part in which:
            next(part, None)

    def swap_edges(ref, lead):
        every = (slice(None),) * lead
        first = ref.at[every + (pl.ds(PAD, HALO),)]
        last = ref.at[every + (pl.ds(PAD + nx - HALO, HALO),)]
        before = ref.at[every + (pl.ds(PAD - HALO, HALO),)]
        after = ref.at[every + (pl.ds(PAD + nx, HALO),)]
        copies = [
            remote(last, before, sems, cols, sec_right),
            remote(first, after, sems, cols, sec_left),
        ]
        for copy in copies:
            copy.start()
            sent.append(copy)
        return copies

    def turn_all(read, write):
        def one(y, carry):
            write(y, turned(read(y), nz))
            return carry

        lax.fori_loop(0, ny, one, 0)

    advance(parts)
    loads[0].wait()
    loads[1].wait()

    def put_d(y, value):
        d_t[y, PAD : PAD + nx, :] = 6.0 * (value - 1.0)

    turn_all(lambda y: potential_v[y], put_d)
    edges = swap_edges(d_t, 1)
    loads[2].wait()
    for column in range(2):
        def put_trial(y, value, column=column):
            trial_t[column, y, PAD : PAD + nx, :] = value

        turn_all(lambda y, column=column: trial_v[column, y], put_trial)
    edges += swap_edges(trial_t, 2)
    advance(parts)
    advance(parts)
    advance(parts)
    for copy in edges:
        copy.wait_recv()

    def field_rows(turn, lo, hi):
        def one(block, carry):
            row = pl.multiple_of(block * 8, 8)
            for y in range(ny):
                value = psi_t[turn][y, pl.ds(row, 8), :]
                for column in range(2):
                    w[column, y, pl.ds(row, 8), :] = value * trial_t[column, y, pl.ds(row, 8), :]
            return carry

        lax.fori_loop(lo, hi, one, 0)

    def step_rows(src, dst, scale, sign, lo, hi):
        def one(block, carry):
            row = pl.multiple_of(8 * lo + block * BLOCK, 8)
            place = pl.ds(row, BLOCK)

            def store(c, y, v):
                base = scale * w[c, y, place, :]
                dst[c, y, place, :] = base + v if sign > 0 else base - v

            for columns in TOGETHER:
                stencil(src, d_t, band_ref[...], columns, ny, row, store)
            return carry

        lax.fori_loop(0, (hi - lo) * 8 // BLOCK, one, 0)

    def last_rows(turn, columns, lo, hi):
        def one(block, carry):
            row = pl.multiple_of(8 * lo + block * BLOCK, 8)
            place = pl.ds(pl.multiple_of(row - PAD, 8), BLOCK)

            def store(c, y, v):
                here = pl.ds(row, BLOCK)
                value = psi_t[turn][y, here, :] * (0.2 * w[c, y, here, :] + v * (1.0 / 864000.0))
                value = value[:, :nz]
                if turn > 0:
                    value = value + total[c, y, place, :]
                total[c, y, place, :] = value

            stencil(u2, d_t, band_ref[...], columns, ny, row, store)
            return carry

        lax.fori_loop(0, (hi - lo) * 8 // BLOCK, one, 0)

    a, b = PAD // 8, (PAD + nx) // 8
    stores = []
    for turn in range(ROUNDS):
        advance(parts[2 * turn : 2 * turn + 2])

        def put_psi(y, value, turn=turn):
            psi_t[turn][y, PAD : PAD + nx, :] = value

        def get_psi(y, turn=turn):
            return psi[turn][pl.ds(pl.multiple_of(y * nz, 8), nz), :]

        turn_all(get_psi, put_psi)
        edges = swap_edges(psi_t[turn], 1)
        field_rows(turn, a, b)
        step_rows(w, u1, 72.0, -1.0, a + 1, b - 1)
        for copy in edges:
            copy.wait_recv()
        field_rows(turn, a - 1, a)
        field_rows(turn, b, b + 1)
        step_rows(w, u1, 72.0, -1.0, a - 1, a + 1)
        step_rows(w, u1, 72.0, -1.0, b - 1, b + 1)
        step_rows(u1, u2, 3600.0, 1.0, a - 1, b + 1)
        for columns in TOGETHER:
            last_rows(turn, columns, a, b)
            if turn == ROUNDS - 1:
                for c in columns:
                    store = pltpu.make_async_copy(total.at[c], out_ref.at[c], store_sem.at[c])
                    store.start()
                    stores.append(store)

    for copy in sent:
        copy.wait_send()
    for store in stores:
        store.wait()


def body(trial, orbitals, potential, owner):
    columns, ny, nz, nx = trial.shape
    n_rows = ny * nz
    tall = PAD + nx + PAD
    xy = X * H
    size_p, size_q = 2 * n_rows // 3, n_rows // 3
    any_spec = pl.BlockSpec(memory_space=pl.ANY)

    def each_round(*shape):
        return (pltpu.VMEM(shape, F32),) * ROUNDS

    n_sems = 4 * ROUNDS * (xy + Z - 2) + 2 * (2 + ROUNDS)
    out = pl.pallas_call(
        kernel,
        out_shape=jax.ShapeDtypeStruct((columns, ny, nx, nz), F32),
        in_specs=[pl.BlockSpec(memory_space=pltpu.SMEM), any_spec, any_spec, any_spec],
        out_specs=any_spec,
        scratch_shapes=[
            pltpu.VMEM(trial.shape, F32),
            pltpu.VMEM((n_rows, nx), F32),
            pltpu.VMEM((ny, nz, nx), F32),
            each_round(n_rows, nx),
            each_round(xy, size_p // xy, nx),
            each_round(Z, size_p // (xy * Z), nx),
            each_round(Z, size_q // Z, nx),
            each_round(xy, size_q // (xy * Z), nx),
            each_round(size_p // xy, nx),
            each_round(size_q // Z, nx),
            each_round(ny, tall, 128),
            pltpu.VMEM((columns, ny, tall, 128), F32),
            pltpu.VMEM((ny, tall, 128), F32),
            pltpu.VMEM((columns, ny, tall, 128), F32),
            pltpu.VMEM((columns, ny, tall, 128), F32),
            pltpu.VMEM((columns, ny, tall, 128), F32),
            pltpu.VMEM((columns, ny, nx, nz), F32),
            pltpu.VMEM((256, 128), jnp.bfloat16),
            pltpu.SemaphoreType.DMA((3,)),
            pltpu.SemaphoreType.DMA((columns,)),
            pltpu.SemaphoreType.DMA((n_sems,)),
            pltpu.SemaphoreType.DMA((n_sems,)),
        ],
        compiler_params=pltpu.CompilerParams(
            collective_id=0, has_side_effects=True, vmem_limit_bytes=60 * 1024 * 1024
        ),
    )(owner, trial, orbitals.reshape(orbitals.shape[0], n_rows, nx), potential)
    return out.transpose(0, 1, 3, 2)


def solution(mesh):
    placed = (P("cols", None, None, "sec"), P("cols", None, None, "sec"), P(None, None, "sec"), P())
    return jax.shard_map(
        body, mesh=mesh, in_specs=placed, out_specs=P("cols", None, None, "sec"), check_vma=False
    )
```

time: 818 us -> 70.6 us (0.09)
  waiting for transfers between devices: 652 us -> 0 us
  other arithmetic: 72.6 us -> 0 us
  Pallas kernels: 0 us -> 67.7 us
  starting transfers between devices: 56.5 us -> 0 us
  local copies, waits for them, and re-layouts: 21.7 us -> 2.78 us
  between operations: 14.8 us -> 0.01 us
    psum x1 -> x0, waiting for transfers between devices: 652 us -> none  [broadcast(): return lax.psum(block, axis)]
    pallas_call x0 -> x1, Pallas kernels: none -> 67.7 us  [body(): pl.pallas_call(kernel, out_shape=jax.ShapeDtypeStruct((columns, ny, nx, n...]
    ppermute x12 -> x0, starting transfers between devices: 56.5 us -> none  [the longest x6 49.7 us: with_halo(): after = lax.ppermute(leading, axis, down)]
    sub x2 -> x0, other arithmetic: 28.4 us -> none  [body(): third = 2.0 * scaled_step(second, potential) - first]
    add x1 -> x0, other arithmetic: 26.4 us -> none  [body(): total = total + occupation * orbital[None] * filtered]
    div x2 -> x0, other arithmetic: 10.4 us -> none  [apply_scaled(): (kinetic + potential * center - spectrum_mid * center) / spectrum_half]
  transfers between devices with their start and end apart: 13 -> 0, of which waited for: 1 -> 0; matrix products, arithmetic and copies ran while one was open for 7% -> 0% of each run, Pallas kernels for 0% -> 0%
where the time goes in v2:
time: 70.6 us; the launch traced here: 70.5 us
  Pallas kernels  67.7 us (96%)
  local copies, waits for them, and re-layouts  2.78 us (4%)
    pallas_call x1, Pallas kernels, body(): pl.pallas_call(kernel, out_shape=jax.ShapeDtypeStruct((columns, ny, nx, n...  67.7 us
    transpose x1, local copies, waits for them, and re-layouts, body(): return out.transpose(0, 1, 3, 2)  2.78 us

profile of v2, /device:TPU:1, one launch (start us, length us, event | category | flops | bytes accessed | tf_op | source)
XLA Modules:
  0.0 70.5 jit_solution(15846093343228135607)
XLA Ops:
  0.0 67.7 %shard_map.46 = f32[2,16,128,96]{3,2,1,0:T(8,128)} custom-call(s32[2]{0:T(128)} %owner_ref.1, f32[2,16,96,128]{3,2,1,0:T(8,128)} %trial_ref.1, f32[1,1536,128]{2,1,0:T(8,128)} %bitcast.3, f32[16,96,128]{2,1,0:T(8,128)} %potential_ref.1), custom_call_target="tpu_custom_call" | custom-call | tf_op jit(solution)/shard_map/pallas_call | solution.py:345
  67.7 2.8 %copy.5 = f32[2,16,96,128]{3,2,1,0:T(8,128)} copy(f32[2,16,96,128]{2,3,1,0:T(8,128)} %bitcast.2) | data formatting | bytes 3145728 | tf_op jit(solution)/shard_map/transpose | solution.py:378

commit v3 on v2

--- a/solution.py
+++ b/solution.py
@@ -12,7 +12,6 @@
 X, Z, H = 4, 8, 2
 PAD = 16
 BLOCK = 16
-TOGETHER = ((0, 1),)
 HALO = 8
 
 
@@ -76,7 +75,6 @@
     def go(src, dst, cols):
         copy = remote(src, dst, sems, cols, sec)
         copy.start()
-        sent.append(copy)
         return copy
 
     def scatter(src, offset, piece, group, landed):
@@ -99,17 +97,19 @@
     piece2 = piece1 // second.size
     inner = base + first.place() * piece1
     copies = scatter(first_copy, base, piece1, first, landed1)
-    yield
+    yield copies
     held[...] = taken(copies, own, base, piece1, first, landed1)
     copies = scatter(held, 0, piece2, second, landed2)
+    sent += copies
     yield
     rows(out, inner + second.place() * piece2, piece2)[...] = taken(copies, held, 0, piece2, second, landed2)
     copies = gather(inner, piece2, second)
+    sent += copies
     yield
     for copy in copies:
         copy.wait_recv()
     copies = gather(base, piece1, first)
-    yield
+    yield copies
     for copy in copies:
         copy.wait_recv()
 
@@ -202,9 +202,8 @@
             )
         )
 
-    def advance(which):
-        for part in which:
-            next(part, None)
+    def advance(turn):
+        return [copy for part in parts[2 * turn : 2 * turn + 2] for copy in next(part, None) or ()]
 
     def swap_edges(ref, lead):
         every = (slice(None),) * lead
@@ -228,27 +227,29 @@
 
         lax.fori_loop(0, ny, one, 0)
 
-    advance(parts)
-    loads[0].wait()
-    loads[1].wait()
-
     def put_d(y, value):
         d_t[y, PAD : PAD + nx, :] = 6.0 * (value - 1.0)
 
+    sent += advance(0) + advance(1)
+    loads[1].wait()
     turn_all(lambda y: potential_v[y], put_d)
-    edges = swap_edges(d_t, 1)
+    edges_in = swap_edges(d_t, 1)
     loads[2].wait()
     for column in range(2):
         def put_trial(y, value, column=column):
             trial_t[column, y, PAD : PAD + nx, :] = value
 
         turn_all(lambda y, column=column: trial_v[column, y], put_trial)
-    edges += swap_edges(trial_t, 2)
-    advance(parts)
-    advance(parts)
-    advance(parts)
-    for copy in edges:
+    edges_in += swap_edges(trial_t, 2)
+    loads[0].wait()
+    for turn in (0, 1, 0, 1):
+        advance(turn)
+    ahead = advance(0)
+    for copy in edges_in:
         copy.wait_recv()
+    for copy in ahead:
+        copy.wait_send()
+    sent += advance(1)
 
     def field_rows(turn, lo, hi):
         def one(block, carry):
@@ -270,8 +271,7 @@
                 base = scale * w[c, y, place, :]
                 dst[c, y, place, :] = base + v if sign > 0 else base - v
 
-            for columns in TOGETHER:
-                stencil(src, d_t, band_ref[...], columns, ny, row, store)
+            stencil(src, d_t, band_ref[...], (0, 1), ny, row, store)
             return carry
 
         lax.fori_loop(0, (hi - lo) * 8 // BLOCK, one, 0)
@@ -295,18 +295,19 @@
         lax.fori_loop(0, (hi - lo) * 8 // BLOCK, one, 0)
 
     a, b = PAD // 8, (PAD + nx) // 8
-    stores = []
-    for turn in range(ROUNDS):
-        advance(parts[2 * turn : 2 * turn + 2])
-
-        def put_psi(y, value, turn=turn):
+
+    def arrive(turn):
+        def put_psi(y, value):
             psi_t[turn][y, PAD : PAD + nx, :] = value
 
-        def get_psi(y, turn=turn):
+        def get_psi(y):
             return psi[turn][pl.ds(pl.multiple_of(y * nz, 8), nz), :]
 
+        advance(turn)
         turn_all(get_psi, put_psi)
-        edges = swap_edges(psi_t[turn], 1)
+        return swap_edges(psi_t[turn], 1)
+
+    def first_two(turn, edges):
         field_rows(turn, a, b)
         step_rows(w, u1, 72.0, -1.0, a + 1, b - 1)
         for copy in edges:
@@ -316,13 +317,17 @@
         step_rows(w, u1, 72.0, -1.0, a - 1, a + 1)
         step_rows(w, u1, 72.0, -1.0, b - 1, b + 1)
         step_rows(u1, u2, 3600.0, 1.0, a - 1, b + 1)
-        for columns in TOGETHER:
-            last_rows(turn, columns, a, b)
-            if turn == ROUNDS - 1:
-                for c in columns:
-                    store = pltpu.make_async_copy(total.at[c], out_ref.at[c], store_sem.at[c])
-                    store.start()
-                    stores.append(store)
+
+    first_two(0, arrive(0))
+    edges = arrive(1)
+    last_rows(0, (0, 1), a, b)
+    first_two(1, edges)
+    stores = []
+    for c in range(2):
+        last_rows(1, (c,), a, b)
+        store = pltpu.make_async_copy(total.at[c], out_ref.at[c], store_sem.at[c])
+        store.start()
+        stores.append(store)
 
     for copy in sent:
         copy.wait_send()

time: 70.6 us -> 69.1 us (0.979)
  Pallas kernels: 67.7 us -> 65.8 us
    pallas_call x1, Pallas kernels: 67.7 us -> 65.8 us  [body(): pl.pallas_call(kernel, out_shape=jax.ShapeDtypeStruct((columns, ny, nx, n...]
where the time goes in v3:
time: 69.1 us; the launch traced here: 68.6 us
  Pallas kernels  65.8 us (95%)
  local copies, waits for them, and re-layouts  2.78 us (4%)
    pallas_call x1, Pallas kernels, body(): pl.pallas_call(kernel, out_shape=jax.ShapeDtypeStruct((columns, ny, nx, n...  65.8 us
    transpose x1, local copies, waits for them, and re-layouts, body(): return out.transpose(0, 1, 3, 2)  2.78 us

profile of v3, /device:TPU:1, one launch (start us, length us, event | category | flops | bytes accessed | tf_op | source)
XLA Modules:
  0.0 68.6 jit_solution(3859020887967870295)
XLA Ops:
  0.0 65.8 %shard_map.46 = f32[2,16,128,96]{3,2,1,0:T(8,128)} custom-call(s32[2]{0:T(128)} %owner_ref.1, f32[2,16,96,128]{3,2,1,0:T(8,128)} %trial_ref.1, f32[1,1536,128]{2,1,0:T(8,128)} %bitcast.3, f32[16,96,128]{2,1,0:T(8,128)} %potential_ref.1), custom_call_target="tpu_custom_call" | custom-call | tf_op jit(solution)/shard_map/pallas_call | solution.py:350
  65.8 2.8 %copy.5 = f32[2,16,96,128]{3,2,1,0:T(8,128)} copy(f32[2,16,96,128]{2,3,1,0:T(8,128)} %bitcast.2) | data formatting | bytes 3145728 | tf_op jit(solution)/shard_map/transpose | solution.py:383

commit v4 on v3

--- a/solution.py
+++ b/solution.py
@@ -11,6 +11,7 @@
 ROUNDS = 2
 X, Z, H = 4, 8, 2
 PAD = 16
+PARTS = 4
 BLOCK = 16
 HALO = 8
 
@@ -225,7 +226,7 @@
             write(y, turned(read(y), nz))
             return carry
 
-        lax.fori_loop(0, ny, one, 0)
+        lax.fori_loop(0, ny, one, 0, unroll=4)
 
     def put_d(y, value):
         d_t[y, PAD : PAD + nx, :] = 6.0 * (value - 1.0)
@@ -323,9 +324,11 @@
     last_rows(0, (0, 1), a, b)
     first_two(1, edges)
     stores = []
-    for c in range(2):
-        last_rows(1, (c,), a, b)
-        store = pltpu.make_async_copy(total.at[c], out_ref.at[c], store_sem.at[c])
+    for part in range(PARTS):
+        tall = nx // PARTS
+        last_rows(1, (0, 1), a + part * tall // 8, a + (part + 1) * tall // 8)
+        window = (slice(None), slice(None), pl.ds(part * tall, tall))
+        store = pltpu.make_async_copy(total.at[window], out_ref.at[window], store_sem.at[part])
         store.start()
         stores.append(store)
 
@@ -372,7 +375,7 @@
             pltpu.VMEM((columns, ny, nx, nz), F32),
             pltpu.VMEM((256, 128), jnp.bfloat16),
             pltpu.SemaphoreType.DMA((3,)),
-            pltpu.SemaphoreType.DMA((columns,)),
+            pltpu.SemaphoreType.DMA((PARTS,)),
             pltpu.SemaphoreType.DMA((n_sems,)),
             pltpu.SemaphoreType.DMA((n_sems,)),
         ],

time: 69.1 us -> 67.2 us (0.973)
  Pallas kernels: 65.8 us -> 64.3 us
    pallas_call x1, Pallas kernels: 65.8 us -> 64.3 us  [body(): pl.pallas_call(kernel, out_shape=jax.ShapeDtypeStruct((columns, ny, nx, n...]
where the time goes in v4:
time: 67.2 us; the launch traced here: 67.1 us
  Pallas kernels  64.3 us (96%)
  local copies, waits for them, and re-layouts  2.78 us (4%)
    pallas_call x1, Pallas kernels, body(): pl.pallas_call(kernel, out_shape=jax.ShapeDtypeStruct((columns, ny, nx, n...  64.3 us
    transpose x1, local copies, waits for them, and re-layouts, body(): return out.transpose(0, 1, 3, 2)  2.78 us

profile of v4, /device:TPU:1, one launch (start us, length us, event | category | flops | bytes accessed | tf_op | source)
XLA Modules:
  0.0 67.1 jit_solution(2672636108956519210)
XLA Ops:
  0.0 64.3 %shard_map.46 = f32[2,16,128,96]{3,2,1,0:T(8,128)} custom-call(s32[2]{0:T(128)} %owner_ref.1, f32[2,16,96,128]{3,2,1,0:T(8,128)} %trial_ref.1, f32[1,1536,128]{2,1,0:T(8,128)} %bitcast.3, f32[16,96,128]{2,1,0:T(8,128)} %potential_ref.1), custom_call_target="tpu_custom_call" | custom-call | tf_op jit(solution)/shard_map/pallas_call | solution.py:353
  64.3 2.8 %copy.5 = f32[2,16,96,128]{3,2,1,0:T(8,128)} copy(f32[2,16,96,128]{2,3,1,0:T(8,128)} %bitcast.2) | data formatting | bytes 3145728 | tf_op jit(solution)/shard_map/transpose | solution.py:386

commit v5 on v4

--- a/solution.py
+++ b/solution.py
@@ -275,7 +275,7 @@
             stencil(src, d_t, band_ref[...], (0, 1), ny, row, store)
             return carry
 
-        lax.fori_loop(0, (hi - lo) * 8 // BLOCK, one, 0)
+        lax.fori_loop(0, (hi - lo) * 8 // BLOCK, one, 0, unroll=2)
 
     def last_rows(turn, columns, lo, hi):
         def one(block, carry):
@@ -293,7 +293,7 @@
             stencil(u2, d_t, band_ref[...], columns, ny, row, store)
             return carry
 
-        lax.fori_loop(0, (hi - lo) * 8 // BLOCK, one, 0)
+        lax.fori_loop(0, (hi - lo) * 8 // BLOCK, one, 0, unroll=2)
 
     a, b = PAD // 8, (PAD + nx) // 8
 

time: 67.2 us -> 63.7 us (0.948)
  Pallas kernels: 64.3 us -> 60.8 us
    pallas_call x1, Pallas kernels: 64.3 us -> 60.8 us  [body(): pl.pallas_call(kernel, out_shape=jax.ShapeDtypeStruct((columns, ny, nx, n...]
where the time goes in v5:
time: 63.7 us; the launch traced here: 63.6 us
  Pallas kernels  60.8 us (95%)
  local copies, waits for them, and re-layouts  2.78 us (4%)
    pallas_call x1, Pallas kernels, body(): pl.pallas_call(kernel, out_shape=jax.ShapeDtypeStruct((columns, ny, nx, n...  60.8 us
    transpose x1, local copies, waits for them, and re-layouts, body(): return out.transpose(0, 1, 3, 2)  2.78 us

profile of v5, /device:TPU:1, one launch (start us, length us, event | category | flops | bytes accessed | tf_op | source)
XLA Modules:
  0.0 63.6 jit_solution(10948587241176512423)
XLA Ops:
  0.0 60.8 %shard_map.46 = f32[2,16,128,96]{3,2,1,0:T(8,128)} custom-call(s32[2]{0:T(128)} %owner_ref.1, f32[2,16,96,128]{3,2,1,0:T(8,128)} %trial_ref.1, f32[1,1536,128]{2,1,0:T(8,128)} %bitcast.3, f32[16,96,128]{2,1,0:T(8,128)} %potential_ref.1), custom_call_target="tpu_custom_call" | custom-call | tf_op jit(solution)/shard_map/pallas_call | solution.py:353
  60.8 2.8 %copy.5 = f32[2,16,96,128]{3,2,1,0:T(8,128)} copy(f32[2,16,96,128]{2,3,1,0:T(8,128)} %bitcast.2) | data formatting | bytes 3145728 | tf_op jit(solution)/shard_map/transpose | solution.py:386

commit v6 on v5

--- a/solution.py
+++ b/solution.py
@@ -254,14 +254,14 @@
 
     def field_rows(turn, lo, hi):
         def one(block, carry):
-            row = pl.multiple_of(block * 8, 8)
+            row = pl.multiple_of(8 * lo + block * 8, 8)
             for y in range(ny):
                 value = psi_t[turn][y, pl.ds(row, 8), :]
                 for column in range(2):
                     w[column, y, pl.ds(row, 8), :] = value * trial_t[column, y, pl.ds(row, 8), :]
             return carry
 
-        lax.fori_loop(lo, hi, one, 0)
+        lax.fori_loop(0, hi - lo, one, 0, unroll=2)
 
     def step_rows(src, dst, scale, sign, lo, hi):
         def one(block, carry):
@@ -275,7 +275,7 @@
             stencil(src, d_t, band_ref[...], (0, 1), ny, row, store)
             return carry
 
-        lax.fori_loop(0, (hi - lo) * 8 // BLOCK, one, 0, unroll=2)
+        lax.fori_loop(0, (hi - lo) * 8 // BLOCK, one, 0, unroll=3)
 
     def last_rows(turn, columns, lo, hi):
         def one(block, carry):

time: 63.7 us -> 63.4 us (level)
  no operation moved by 1% of the time
where the time goes in v6:
time: 63.4 us; the launch traced here: 63.3 us
  Pallas kernels  60.5 us (95%)
  local copies, waits for them, and re-layouts  2.78 us (4%)
    pallas_call x1, Pallas kernels, body(): pl.pallas_call(kernel, out_shape=jax.ShapeDtypeStruct((columns, ny, nx, n...  60.5 us
    transpose x1, local copies, waits for them, and re-layouts, body(): return out.transpose(0, 1, 3, 2)  2.78 us

profile of v6, /device:TPU:1, one launch (start us, length us, event | category | flops | bytes accessed | tf_op | source)
XLA Modules:
  0.0 63.3 jit_solution(16203807917232706344)
XLA Ops:
  0.0 60.5 %shard_map.46 = f32[2,16,128,96]{3,2,1,0:T(8,128)} custom-call(s32[2]{0:T(128)} %owner_ref.1, f32[2,16,96,128]{3,2,1,0:T(8,128)} %trial_ref.1, f32[1,1536,128]{2,1,0:T(8,128)} %bitcast.3, f32[16,96,128]{2,1,0:T(8,128)} %potential_ref.1), custom_call_target="tpu_custom_call" | custom-call | tf_op jit(solution)/shard_map/pallas_call | solution.py:353
  60.5 2.8 %copy.5 = f32[2,16,96,128]{3,2,1,0:T(8,128)} copy(f32[2,16,96,128]{2,3,1,0:T(8,128)} %bitcast.2) | data formatting | bytes 3145728 | tf_op jit(solution)/shard_map/transpose | solution.py:386
